TPU v7x, 32 devices: a whole 2x2x4 slice. The times are simulated.
32 devices in a mesh: beam: 2 (over y), freq: 8 (over z, x), section: 2 (over core).
Axes of the slice: x: 2, y: 2, z: 4, core: 2. Of those that a mesh axis runs over, the one named last changes fastest.
Arguments:
- voltages: int32 [256, 8, 2, 1024], P(('beam', 'freq', 'section')), parts along dimension 0, may hold values from -7 to 7, as said below
- filter_taps: float32 [8, 1024], replicated, may hold values from -0.0625 to 0.0625
- delay_plan: int32 [2, 28672], replicated, may hold values from 0 to 1023
Outputs:
- dedispersed: float32 [4096, 128], P(('beam', 'freq', 'section')), parts along dimension 0
There are 2 independent parts, one for each index of `beam`. A program takes and returns all parts, laid end to end along the dimension named above; an argument that names none is the same for every part. Nothing has to cross between parts.
Inputs may be any that keep to these rules, and one draw needn't show every extreme that they name: `voltages`: quantised samples; dimension 2 holds the real and imaginary parts.
All inputs are finite; a program needn't handle non-finite values.
Results may differ from a plain program's by a relative error of at most 0.0003.
Values may be sent and summed in bfloat16 or wider, within the bound.
A program may use at most 64 MiB of HBM per device.

v0:
```python
import math

import jax
import jax.numpy as jnp
import numpy as np
from jax import lax
from jax.sharding import PartitionSpec as P

NDELAY = 2048


EPSILON = 1e-05


def shifted(value, axis, steps):
    count = lax.axis_size(axis)
    leading, last = (max(0, -steps), min(count, count - steps))
    return lax.ppermute(value, axis, [(source, source + steps) for source in range(leading, last)])


def swapped(value, axis, apart):
    return lax.ppermute(value, axis, [(i, i ^ 1 << apart) for i in range(lax.axis_size(axis))])


def dft_table(length):
    index_row = jnp.arange(length, dtype=jnp.int32)
    phase = index_row[:, None] * (index_row[None, :] - length // 2) % length
    angle = phase.astype(jnp.float32) * jnp.float32(2.0 * math.pi / length)
    cosine = jnp.cos(angle).astype(jnp.bfloat16)
    sine = jnp.sin(angle).astype(jnp.bfloat16)
    real_rows = jnp.concatenate([cosine, -sine], axis=1)
    imag_rows = jnp.concatenate([sine, cosine], axis=1)
    return jnp.concatenate([real_rows, imag_rows], axis=0)


def delayed(source_rows, shift):
    span_width = source_rows.shape[1]
    padded = jnp.concatenate([source_rows, jnp.zeros_like(source_rows)], axis=1)
    return jax.vmap(lambda one_row, start: lax.dynamic_slice_in_dim(one_row, start, span_width))(
        padded, shift
    )


def merge_rows(state, shift, upper_rows, lower_rows):
    return jnp.take(state, upper_rows, axis=0) + delayed(jnp.take(state, lower_rows, axis=0), shift)


def reversed_bits(value, bit_count):
    result = jnp.zeros_like(value)
    for bit_index in range(bit_count):
        single = jnp.bitwise_and(jnp.right_shift(value, bit_index), 1)
        result = result + jnp.left_shift(single, bit_count - 1 - bit_index)
    return result


def static_reversal(count, bit_count):
    listing = []
    for entry in range(count):
        listing.append(
            sum(
                (
                    (entry >> bit_index & 1) << bit_count - 1 - bit_index
                    for bit_index in range(bit_count)
                )
            )
        )
    return np.array(listing, dtype=np.int32)


def per_device(voltages, filter_taps, delay_plan):
    devices = lax.axis_size(("freq", "section"))
    position = lax.axis_index(("freq", "section"))
    merges = devices.bit_length() - 1
    frames_dev = voltages.shape[0]
    coarse = voltages.shape[1]
    fft_length = voltages.shape[3]
    tap_count = filter_taps.shape[0]
    channels = coarse * fft_length
    frames = frames_dev * devices
    delays = NDELAY
    delay_block = delays // devices
    flat_levels = (channels // delays).bit_length() - 1
    local_levels = (channels // devices).bit_length() - 1
    anchor = reversed_bits(position, merges)
    block_order = static_reversal(devices, merges)
    samples = voltages.astype(jnp.bfloat16)
    prior = shifted(samples[frames_dev - tap_count + 1 :], ("freq", "section"), 1)
    extended = jnp.concatenate([prior, samples], axis=0)
    summed = extended[0:frames_dev].astype(jnp.float32) * filter_taps[0]
    for tap_index in range(1, tap_count):
        summed = (
            summed
            + extended[tap_index : tap_index + frames_dev].astype(jnp.float32)
            * filter_taps[tap_index]
        )
    filtered = summed.astype(jnp.bfloat16).reshape(frames_dev * coarse, 2 * fft_length)
    spectra = jnp.dot(filtered, dft_table(fft_length), preferred_element_type=jnp.float32)
    real_part = spectra[:, :fft_length]
    imag_part = spectra[:, fft_length:]
    power = (
        (real_part * real_part + imag_part * imag_part)
        .astype(jnp.bfloat16)
        .reshape(frames_dev, channels)
    )
    grouped = jnp.take(power.reshape(frames_dev, devices, channels // devices), block_order, axis=1)
    turned = lax.all_to_all(
        grouped.reshape(frames_dev, channels),
        ("freq", "section"),
        split_axis=1,
        concat_axis=0,
        tiled=True,
    )
    series = turned.astype(jnp.float32).T
    mean = jnp.mean(series, axis=1, keepdims=True)
    centered = series - mean
    variance = jnp.mean(centered * centered, axis=1, keepdims=True)
    normed = centered / jnp.sqrt(channels * (variance + EPSILON))
    state = jnp.sum(normed.reshape(-1, 2**flat_levels, frames), axis=1)
    row_index = jnp.arange(delay_block, dtype=jnp.int32)

    def local_level(level, current):
        width = jnp.left_shift(jnp.int32(1), level - flat_levels)
        half_width = width // 2
        band_index = row_index // width
        start = channels - delays + (level - flat_levels - 1) * delays + anchor * delay_block
        upper = lax.dynamic_slice_in_dim(delay_plan[0], start, delay_block)
        lower = lax.dynamic_slice_in_dim(delay_plan[1], start, delay_block)
        return merge_rows(
            current,
            upper,
            (2 * band_index + 1) * half_width + upper,
            2 * band_index * half_width + lower,
        )

    state = lax.fori_loop(flat_levels + 1, local_levels + 1, local_level, state)
    for step in range(merges):
        bit_place = merges - 1 - step
        side = jnp.bitwise_and(jnp.right_shift(position, bit_place), 1)
        column = jnp.right_shift(position, bit_place + 1)
        level = local_levels + step + 1
        width = delay_block * 2 ** (step + 1)
        start = channels - delays + (level - flat_levels - 1) * delays
        start = (
            start + jnp.right_shift(anchor, step + 1) * width + (2 * column + side) * delay_block
        )
        upper = lax.dynamic_slice_in_dim(delay_plan[0], start, delay_block)
        lower = lax.dynamic_slice_in_dim(delay_plan[1], start, delay_block)
        other = swapped(state, ("freq", "section"), bit_place)
        low_tile = jnp.where(side == 0, state, other)
        high_tile = jnp.where(side == 0, other, state)
        row_base = column * delay_block
        state = jnp.take(high_tile, upper - row_base, axis=0) + delayed(
            jnp.take(low_tile, lower - row_base, axis=0), upper
        )
    return state


def solution(mesh):
    placed = (P(("beam", "freq", "section"), None, None, None), P(), P())
    return jax.shard_map(
        per_device,
        mesh=mesh,
        in_specs=placed,
        out_specs=P(("beam", "freq", "section"), None),
        check_vma=False,
    )
```

profile of v0, /device:TPU:0, one launch (start us, length us, event | category | flops | bytes accessed | tf_op | source)
XLA Modules:
  0.0 2883.5 jit_solution(16114216390199819055)
XLA Ops:
  1.4 2.4 collective-permute-start
  3.8 18.0 sine_convert_fusion
  21.8 16.9 fusion.18
  39.1 2.2 fusion.29
  41.4 12.5 fusion.4
  55.3 7.2 all-to-all-start
  62.6 7.9 all-to-all-done
  70.9 1720.3 %while.33 = (s32[]{:T(128)}, f32[128,128]{1,0:T(8,128)S(1)}, s32[2,28672]{1,0:T(2,128)S(1)}, s32[]{:T(128)}, s32[]{:T(128)}, /*index=5*/s32[]{:T(128)}, s32[]{:T...) while((s32[]{:T(128)}, f32[128,128]{1,0:T(8,128)S(1)}, ...), condition=%wide.region_4.6_spmd.clone.clone, body=%wide.region_3.5_spmd.clone.clone.sunk | while | flops 55195 | bytes 1264198 | solution.py:135
  72.1 243.8 %while.34 = (s32[]{:T(128)}, f32[128,256]{1,0:T(8,128)S(1)}, s32[128,2]{0,1:T(2,128)S(1)}, f32[128,128]{1,0:T(8,128)S(1)}, s32[]{:T(128)}, /*index=5*/s32[]{:T(128)}) while((s32[]{:T(128)}, f32[128,256]{1,0:T(8,128)S(1)}, s32[128,2]{0,1:T(2,128)S(1)}, f32[128,128]{1,0:T(8,128)S(1)}, s32[]{:T(128)}, /*index=5*/s32[]{:T(128)}) %tuple.186), condition=%wide.while_cond, body=%wide.while_body.sunk | while | flops 2 | bytes 2161 | solution.py:39
  317.9 243.8 %while.34 = (s32[]{:T(128)}, f32[128,256]{1,0:T(8,128)S(1)}, s32[128,2]{0,1:T(2,128)S(1)}, f32[128,128]{1,0:T(8,128)S(1)}, s32[]{:T(128)}, /*index=5*/s32[]{:T(128)}) while((s32[]{:T(128)}, f32[128,256]{1,0:T(8,128)S(1)}, s32[128,2]{0,1:T(2,128)S(1)}, f32[128,128]{1,0:T(8,128)S(1)}, s32[]{:T(128)}, /*index=5*/s32[]{:T(128)}) %tuple.186), condition=%wide.while_cond, body=%wide.while_body.sunk | while | flops 2 | bytes 2161 | solution.py:39
  563.6 243.8 %while.34 = (s32[]{:T(128)}, f32[128,256]{1,0:T(8,128)S(1)}, s32[128,2]{0,1:T(2,128)S(1)}, f32[128,128]{1,0:T(8,128)S(1)}, s32[]{:T(128)}, /*index=5*/s32[]{:T(128)}) while((s32[]{:T(128)}, f32[128,256]{1,0:T(8,128)S(1)}, s32[128,2]{0,1:T(2,128)S(1)}, f32[128,128]{1,0:T(8,128)S(1)}, s32[]{:T(128)}, /*index=5*/s32[]{:T(128)}) %tuple.186), condition=%wide.while_cond, body=%wide.while_body.sunk | while | flops 2 | bytes 2161 | solution.py:39
  809.4 243.8 %while.34 = (s32[]{:T(128)}, f32[128,256]{1,0:T(8,128)S(1)}, s32[128,2]{0,1:T(2,128)S(1)}, f32[128,128]{1,0:T(8,128)S(1)}, s32[]{:T(128)}, /*index=5*/s32[]{:T(128)}) while((s32[]{:T(128)}, f32[128,256]{1,0:T(8,128)S(1)}, s32[128,2]{0,1:T(2,128)S(1)}, f32[128,128]{1,0:T(8,128)S(1)}, s32[]{:T(128)}, /*index=5*/s32[]{:T(128)}) %tuple.186), condition=%wide.while_cond, body=%wide.while_body.sunk | while | flops 2 | bytes 2161 | solution.py:39
  1055.1 243.8 %while.34 = (s32[]{:T(128)}, f32[128,256]{1,0:T(8,128)S(1)}, s32[128,2]{0,1:T(2,128)S(1)}, f32[128,128]{1,0:T(8,128)S(1)}, s32[]{:T(128)}, /*index=5*/s32[]{:T(128)}) while((s32[]{:T(128)}, f32[128,256]{1,0:T(8,128)S(1)}, s32[128,2]{0,1:T(2,128)S(1)}, f32[128,128]{1,0:T(8,128)S(1)}, s32[]{:T(128)}, /*index=5*/s32[]{:T(128)}) %tuple.186), condition=%wide.while_cond, body=%wide.while_body.sunk | while | flops 2 | bytes 2161 | solution.py:39
  1300.9 243.8 %while.34 = (s32[]{:T(128)}, f32[128,256]{1,0:T(8,128)S(1)}, s32[128,2]{0,1:T(2,128)S(1)}, f32[128,128]{1,0:T(8,128)S(1)}, s32[]{:T(128)}, /*index=5*/s32[]{:T(128)}) while((s32[]{:T(128)}, f32[128,256]{1,0:T(8,128)S(1)}, s32[128,2]{0,1:T(2,128)S(1)}, f32[128,128]{1,0:T(8,128)S(1)}, s32[]{:T(128)}, /*index=5*/s32[]{:T(128)}) %tuple.186), condition=%wide.while_cond, body=%wide.while_body.sunk | while | flops 2 | bytes 2161 | solution.py:39
  1546.7 243.8 %while.34 = (s32[]{:T(128)}, f32[128,256]{1,0:T(8,128)S(1)}, s32[128,2]{0,1:T(2,128)S(1)}, f32[128,128]{1,0:T(8,128)S(1)}, s32[]{:T(128)}, /*index=5*/s32[]{:T(128)}) while((s32[]{:T(128)}, f32[128,256]{1,0:T(8,128)S(1)}, s32[128,2]{0,1:T(2,128)S(1)}, f32[128,128]{1,0:T(8,128)S(1)}, s32[]{:T(128)}, /*index=5*/s32[]{:T(128)}) %tuple.186), condition=%wide.while_cond, body=%wide.while_body.sunk | while | flops 2 | bytes 2161 | solution.py:39
  1791.7 5.2 collective-permute-done.1
  1797.7 267.5 %while.28 = (s32[]{:T(128)}, f32[128,256]{1,0:T(8,128)S(1)}, s32[128,2]{0,1:T(2,128)S(1)}, f32[128,128]{1,0:T(8,128)S(1)}, s32[]{:T(128)}, /*index=5*/s32[]{:T(128)}) while((s32[]{:T(128)}, f32[128,256]{1,0:T(8,128)S(1)}, s32[128,2]{0,1:T(2,128)S(1)}, f32[128,128]{1,0:T(8,128)S(1)}, s32[]{:T(128)}, /*index=5*/s32[]{:T(128)}) %tuple.192), condition=%wide.while_cond.1, body=%wide.while_body.1.sunk | while | flops 2 | bytes 2161 | solution.py:39
  1800.5 1.4 dynamic-slice.59
  1802.6 1.4 dynamic-slice.59
  1804.7 1.4 dynamic-slice.59
  1808.9 1.4 dynamic-slice.59
  1810.9 1.4 dynamic-slice.59
  1815.1 1.4 dynamic-slice.59
  1817.2 1.4 dynamic-slice.59
  1821.4 1.4 dynamic-slice.59
  1823.5 1.4 dynamic-slice.59
  1827.7 1.4 dynamic-slice.59
  1829.7 1.4 dynamic-slice.59
  1833.9 1.4 dynamic-slice.59
  1836.0 1.4 dynamic-slice.59
  1840.2 1.4 dynamic-slice.59
  1842.3 1.4 dynamic-slice.59
  1844.4 1.4 dynamic-slice.59
  1848.6 1.4 dynamic-slice.59
  1850.6 1.4 dynamic-slice.59
  1854.8 1.4 dynamic-slice.59
  1856.9 1.4 dynamic-slice.59
  1861.1 1.4 dynamic-slice.59
  1863.2 1.4 dynamic-slice.59
  1867.4 1.4 dynamic-slice.59
  1869.4 1.4 dynamic-slice.59
  1873.6 1.4 dynamic-slice.59
  1875.7 1.4 dynamic-slice.59
  2066.0 4.2 collective-permute-done.2
  2071.0 267.5 %while.29 = (s32[]{:T(128)}, f32[128,256]{1,0:T(8,128)S(1)}, s32[128,2]{0,1:T(2,128)S(1)}, f32[128,128]{1,0:T(8,128)S(1)}, s32[]{:T(128)}, /*index=5*/s32[]{:T(128)}) while((s32[]{:T(128)}, f32[128,256]{1,0:T(8,128)S(1)}, s32[128,2]{0,1:T(2,128)S(1)}, f32[128,128]{1,0:T(8,128)S(1)}, s32[]{:T(128)}, /*index=5*/s32[]{:T(128)}) %tuple.195), condition=%wide.while_cond.2, body=%wide.while_body.2.sunk | while | flops 2 | bytes 2161 | solution.py:39
  2340.0 3.6 collective-permute-done.3
  2344.4 267.5 %while.30 = (s32[]{:T(128)}, f32[128,256]{1,0:T(8,128)S(1)}, s32[128,2]{0,1:T(2,128)S(1)}, f32[128,128]{1,0:T(8,128)S(1)}, s32[]{:T(128)}, /*index=5*/s32[]{:T(128)}) while((s32[]{:T(128)}, f32[128,256]{1,0:T(8,128)S(1)}, s32[128,2]{0,1:T(2,128)S(1)}, f32[128,128]{1,0:T(8,128)S(1)}, s32[]{:T(128)}, /*index=5*/s32[]{:T(128)}) %tuple.198), condition=%wide.while_cond.3, body=%wide.while_body.3.sunk | while | flops 2 | bytes 2161 | solution.py:39
  2614.7 267.5 %while.31 = (s32[]{:T(128)}, f32[128,256]{1,0:T(8,128)S(1)}, s32[128,2]{0,1:T(2,128)S(1)}, f32[128,128]{1,0:T(8,128)S(1)}, s32[]{:T(128)}, /*index=5*/s32[]{:T(128)}) while((s32[]{:T(128)}, f32[128,256]{1,0:T(8,128)S(1)}, s32[128,2]{0,1:T(2,128)S(1)}, f32[128,128]{1,0:T(8,128)S(1)}, s32[]{:T(128)}, /*index=5*/s32[]{:T(128)}) %tuple.201), condition=%wide.while_cond.4, body=%wide.while_body.4.sunk | while | flops 2 | bytes 2161 | solution.py:39
  (5767 shorter events, 2761.4 us)
Async XLA Ops:
  1.4 37.7 %collective-permute-start = (bf16[7,8,2,1024]{3,2,1,0:T(2,128)(2,1)S(1)}, bf16[7,8,2,1024]{3,2,1,0:T(2,128)(2,1)S(1)}, u32[]{:S(2)}, u32[]{:S(2)}) collective-permute-start(bf16[7,8,2,1024]{3,2,1,0:T(2,128)(2,1)S(1)} %slice.190), channel_id=1, source_target_pairs={{0,1},{1,2},{2,3},{3,4},{4,5},{5,6},{6,7},{7,8},{8,9},{9,10},{10,1... | collective-permute-start | bytes 688136 | tf_op jit(solution)/shard_map/ppermute | solution.py:18
  21.8 16.9 copy-start.2
  21.8 17.0 copy-start
  21.8 17.2 copy-start.1
  55.3 15.1 all-to-all-start
  1791.2 5.7 collective-permute-start.1
  2065.9 4.3 collective-permute-start.2
  2339.2 4.3 collective-permute-start.3
  2612.6 1.3 collective-permute-start.4
where the time goes:
time: 2930 us; the launch traced here: 2880 us
  local copies, waits for them, and re-layouts  2790 us (95%)
  other arithmetic  42.6 us (1%)
    gather x5632, local copies, waits for them, and re-layouts  2770 us

commit v1 on v0

v1 whole, which is shorter than its diff:
```python
import functools
import math

import jax
import jax.numpy as jnp
import numpy as np
from jax import lax
from jax.experimental import pallas as pl
from jax.experimental.pallas import tpu as pltpu
from jax.sharding import PartitionSpec as P

NDELAY = 2048

EPSILON = 1e-05

LANES = 128
TILE = 8
COLUMNS = 256
MESH = pl.DeviceIdType.MESH


def dft_columns(length, chunk, flat):
    wide = chunk // flat
    place = np.arange(length)
    channel = place // chunk * chunk + place % wide * flat + place % chunk // wide
    phase = np.arange(length)[:, None] * (channel[None, :] - length // 2) % length
    angle = phase.astype(np.float32) * np.float32(2.0 * math.pi / length)
    cosine = np.cos(angle).astype(jnp.bfloat16).reshape(length, -1, COLUMNS)
    sine = np.sin(angle).astype(jnp.bfloat16).reshape(length, -1, COLUMNS)
    return np.ascontiguousarray(np.concatenate([cosine, sine], axis=2).transpose(1, 0, 2))


class Sizes:
    def __init__(self, voltages, taps, devices, sections):
        self.devices, self.sections = devices, sections
        self.frames_dev, self.coarse, _, self.length = voltages.shape
        self.taps = taps.shape[0]
        self.channels = self.coarse * self.length
        self.frames = self.frames_dev * devices
        self.merges = devices.bit_length() - 1
        self.levels = self.channels.bit_length() - 1
        self.flat_levels = (self.channels // NDELAY).bit_length() - 1
        self.flat = 1 << self.flat_levels
        self.local_levels = self.levels - self.merges
        self.block = NDELAY // devices
        own = self.channels // devices
        self.chunk = max(own, LANES * self.flat)
        self.share = self.chunk // own
        self.spans = self.frames // LANES
        self.held = {self.levels: self.block // TILE}
        for level in range(self.levels, self.local_levels, -1):
            self.held[level - 1] = max(1, self.held[level] // 2)

    def width(self, level):
        return max(1, NDELAY * 2**level // self.channels)

    def offset(self, level):
        return sum((self.channels >> m) * self.width(m) for m in range(1, level))

    def first_tile(self, device, level):
        tile, held = device * self.held[self.levels], self.held[self.levels]
        for _ in range(self.levels - level):
            tile = tile // 2
        return tile

    def pieces(self, me):
        found = []
        for level in range(self.flat_levels + 1, self.local_levels + 1):
            found.append((level, self.offset(level) + me * self.block, self.block // TILE))
        for level in range(self.local_levels + 1, self.levels + 1):
            for band in range(self.channels >> level):
                start = self.offset(level) + band * self.width(level)
                found.append((level, start + TILE * self.first_tile(me, level), self.held[level]))
        return found


def picked(tile, rows):
    return jnp.concatenate(
        [
            jnp.take_along_axis(
                tile[:, at : at + LANES], rows, axis=0, mode="promise_in_bounds"
            )
            for at in range(0, tile.shape[1], LANES)
        ],
        axis=1,
    )


def later(tile, shift):
    place = lax.broadcasted_iota(jnp.int32, shift.shape, 1) + shift
    inside, span = place & (LANES - 1), place // LANES
    spans = tile.shape[1] // LANES
    turned = [
        jnp.take_along_axis(
            tile[:, s * LANES : (s + 1) * LANES], inside, axis=1, mode="promise_in_bounds"
        )
        for s in range(spans)
    ]
    result = []
    for out in range(spans):
        total = jnp.where(span == 0, turned[out], 0.0)
        for s in range(out + 1, spans):
            total = jnp.where(span == s - out, turned[s], total)
        result.append(total)
    return jnp.concatenate(result, axis=1)


def kernel(
    z,
    axes,
    x_ref,
    taps_ref,
    plan_ref,
    table_ref,
    out_ref,
    table,
    halo,
    lhs,
    power,
    outgoing,
    series,
    turned,
    flat,
    state,
    tiles_in,
    plan_rows,
    plan_columns,
    upper_plan,
    lower_plan,
    table_sem,
    halo_sem,
    send_sem,
    recv_sem,
    send2_sem,
    recv2_sem,
):
    beam = lax.axis_index(axes[0])
    me = lax.axis_index(axes[1]) * z.sections + lax.axis_index(axes[2])

    def at(device):
        return (beam, device // z.sections, lax.rem(device, z.sections))

    loads = []
    for part in range(table_ref.shape[0]):
        loads.append(
            pltpu.make_async_copy(table_ref.at[part], table.at[part], table_sem.at[part])
        )
        loads[-1].start()

    barrier = pltpu.get_barrier_semaphore()

    def greet(step, carry):
        pl.semaphore_signal(
            barrier, inc=1, device_id=at(lax.rem(me + step, z.devices)), device_id_type=MESH
        )
        return carry

    lax.fori_loop(1, z.devices, greet, 0)
    pl.semaphore_wait(barrier, z.devices - 1)

    before = z.taps - 1
    ahead = pltpu.make_async_remote_copy(
        src_ref=x_ref.at[pl.ds(z.frames_dev - before, before)],
        dst_ref=halo,
        send_sem=halo_sem.at[0],
        recv_sem=halo_sem.at[1],
        device_id=at(lax.rem(me + 1, z.devices)),
        device_id_type=MESH,
    )

    @pl.when(me < z.devices - 1)
    def _():
        ahead.start()

    @pl.when(me == 0)
    def _():
        halo[...] = jnp.zeros_like(halo)

    pieces = z.pieces(me)
    plan_rows[...] = jnp.zeros_like(plan_rows)
    for piece, (_, start, _) in enumerate(pieces):
        base = pl.multiple_of(start // LANES * LANES, LANES)
        plan_rows[2 * piece : 2 * piece + 2, :] = plan_ref[:, pl.ds(base, LANES)]
    for row in range(0, plan_rows.shape[0], LANES):
        plan_columns[:, row : row + LANES] = plan_rows[row : row + LANES, :].T
    entry = 0
    for piece, (_, start, count) in enumerate(pieces):
        for tile in range(count):
            row = pl.multiple_of(lax.rem(start, LANES) + TILE * tile, TILE)
            both = plan_columns[pl.ds(row, TILE), 2 * piece : 2 * piece + 2]
            upper_plan[entry] = jnp.broadcast_to(both[:, 0:1], (TILE, LANES))
            lower_plan[entry] = jnp.broadcast_to(both[:, 1:2], (TILE, LANES))
            entry += 1

    @pl.when(me > 0)
    def _():
        ahead.wait_recv()

    half = z.coarse
    rows = z.frames_dev * z.coarse
    for lane in range(0, z.length, LANES):
        lanes = slice(lane, lane + LANES)
        window = [halo[n, :, lanes].astype(jnp.float32) for n in range(before)]
        window += [x_ref[n, :, lanes].astype(jnp.float32) for n in range(z.frames_dev)]
        taps = [taps_ref[j : j + 1, lanes] for j in range(z.taps)]
        summed = []
        for n in range(z.frames_dev):
            total = window[n] * taps[0]
            for j in range(1, z.taps):
                total = total + window[n + j] * taps[j]
            summed.append(total)
        for part in range(2):
            for n in range(0, z.frames_dev, 2):
                own = slice(part * half, (part + 1) * half)
                pair = jnp.concatenate([summed[n][own], summed[n + 1][own]], axis=0)
                first = part * rows + n * half
                lhs[first : first + 2 * half, lanes] = pair.astype(jnp.bfloat16)

    per_coarse = z.length // z.chunk
    parts = z.chunk // COLUMNS
    side = z.chunk // 2

    def parcel(chunk, device):
        return pltpu.make_async_remote_copy(
            src_ref=outgoing.at[chunk],
            dst_ref=series.at[me],
            send_sem=send_sem.at[device],
            recv_sem=recv_sem.at[me],
            device_id=at(device),
            device_id_type=MESH,
        )

    for position in range(per_coarse):
        for part in range(parts):
            index = position * parts + part
            loads[index].wait()
            product = jnp.dot(lhs[...], table[index], preferred_element_type=jnp.float32)
            real = product[:rows, :COLUMNS] + product[rows:, COLUMNS:]
            imag = product[rows:, :COLUMNS] - product[:rows, COLUMNS:]
            squared = real * real + imag * imag
            for lane in range(0, COLUMNS, LANES):
                power[(part * COLUMNS + lane) // LANES] = squared[:, lane : lane + LANES]
        for c in range(z.coarse):
            found = [
                power[k, pl.ds(c, z.frames_dev, stride=z.coarse), :]
                for k in range(z.chunk // LANES)
            ]
            many = len(found) // 2
            for k in range(many):
                outgoing[c * per_coarse + position, :, k * LANES : (k + 1) * LANES] = (
                    jnp.concatenate([found[k], found[many + k]], axis=0).astype(jnp.bfloat16)
                )

        def send(step, carry):
            c = lax.rem(step + me // (z.share * per_coarse), z.coarse)
            chunk = c * per_coarse + position
            for twin in range(z.share):
                device = chunk * z.share + twin

                @pl.when(device != me)
                def _():
                    parcel(chunk, device).start()

            return carry

        lax.fori_loop(0, z.coarse, send, 0)
    series[me] = outgoing[me // z.share]

    def receive(step, carry):
        source = lax.rem(me + step, z.devices)
        pltpu.make_async_remote_copy(
            src_ref=outgoing.at[0],
            dst_ref=series.at[source],
            send_sem=send_sem.at[source],
            recv_sem=recv_sem.at[source],
            device_id=at(source),
            device_id_type=MESH,
        ).wait_recv()
        return carry

    lax.fori_loop(1, z.devices, receive, 0)

    rows8 = z.frames_dev
    values = []
    for d in range(z.devices):
        both = series[d].astype(jnp.float32)
        values.append((both[:rows8], both[rows8:]))
    centred = []
    for k in range(2):
        total = values[0][k]
        for d in range(1, z.devices):
            total = total + values[d][k]
        mean = jnp.sum(total, axis=0, keepdims=True) * (1.0 / z.frames)
        part = [values[d][k] - mean for d in range(z.devices)]
        total = part[0] * part[0]
        for d in range(1, z.devices):
            total = total + part[d] * part[d]
        variance = jnp.sum(total, axis=0, keepdims=True) * (1.0 / z.frames)
        scale = 1.0 / jnp.sqrt(z.channels * (variance + EPSILON))
        centred.append((part, scale))
    wide = z.chunk // z.flat
    for d in range(z.devices):
        total = None
        for k in range(2):
            part, scale = centred[k]
            normed = part[d] * scale
            for lane in range(0, side, wide):
                piece = normed[:, lane : lane + wide]
                total = piece if total is None else total + piece
        turned[d * rows8 : (d + 1) * rows8, :] = total
    for span in range(z.spans):
        lanes = slice(span * LANES, (span + 1) * LANES)
        flat[:, lanes] = turned[lanes, :].T

    mine = pl.multiple_of(lax.rem(me, z.share) * z.block, TILE)
    tiles = [
        flat[pl.ds(pl.multiple_of(mine + TILE * k, TILE), TILE), :]
        for k in range(z.block // TILE)
    ]
    entry = 0
    row_in_tile = lax.broadcasted_iota(jnp.int32, (TILE, LANES), 0)
    for level in range(z.flat_levels + 1, z.local_levels + 1):
        width = z.width(level)
        merged = []
        for k in range(len(tiles)):
            h, g = upper_plan[entry], lower_plan[entry]
            entry += 1
            if width <= TILE:
                base = row_in_tile // width * width
                high, low = tiles[k], tiles[k]
                high_rows, low_rows = base + width // 2 + h, base + g
            else:
                many = width // TILE
                first = k // many * many + k % many // 2
                high, low = tiles[first + many // 2], tiles[first]
                high_rows, low_rows = h & (TILE - 1), g & (TILE - 1)
            merged.append(picked(high, high_rows) + later(picked(low, low_rows), h))
        tiles = merged
    for k, tile in enumerate(tiles):
        state[k] = tile

    def deliver(step, carry):
        device = lax.rem(me + step, z.devices)
        pltpu.make_async_remote_copy(
            src_ref=state.at[z.first_tile(device, z.local_levels)],
            dst_ref=tiles_in.at[me],
            send_sem=send2_sem.at[device],
            recv_sem=recv2_sem.at[me],
            device_id=at(device),
            device_id_type=MESH,
        ).start()
        return carry

    lax.fori_loop(1, z.devices, deliver, 0)
    tiles_in[me] = state[z.first_tile(me, z.local_levels)]

    def accept(step, carry):
        source = lax.rem(me + step, z.devices)
        pltpu.make_async_remote_copy(
            src_ref=state.at[0],
            dst_ref=tiles_in.at[source],
            send_sem=send2_sem.at[source],
            recv_sem=recv2_sem.at[source],
            device_id=at(source),
            device_id_type=MESH,
        ).wait_recv()
        return carry

    lax.fori_loop(1, z.devices, accept, 0)

    bands = [[tiles_in[d]] for d in range(z.devices)]
    for level in range(z.local_levels + 1, z.levels + 1):
        merged = []
        for band in range(len(bands) // 2):
            result = []
            for k in range(z.held[level]):
                h, g = upper_plan[entry], lower_plan[entry]
                entry += 1
                high = picked(bands[2 * band + 1][k // 2], h & (TILE - 1))
                low = picked(bands[2 * band][k // 2], g & (TILE - 1))
                result.append(high + later(low, h))
            merged.append(result)
        bands = merged
    for k, tile in enumerate(bands[0]):
        out_ref[k * TILE : (k + 1) * TILE, :] = tile

    @pl.when(me < z.devices - 1)
    def _():
        ahead.wait_send()

    def finish(step, carry):
        device = lax.rem(me + step, z.devices)
        pltpu.make_async_remote_copy(
            src_ref=outgoing.at[0],
            dst_ref=series.at[0],
            send_sem=send_sem.at[device],
            recv_sem=recv_sem.at[device],
            device_id=at(device),
            device_id_type=MESH,
        ).wait_send()
        pltpu.make_async_remote_copy(
            src_ref=state.at[0],
            dst_ref=tiles_in.at[0],
            send_sem=send2_sem.at[device],
            recv_sem=recv2_sem.at[device],
            device_id=at(device),
            device_id_type=MESH,
        ).wait_send()
        return carry

    lax.fori_loop(1, z.devices, finish, 0)


def per_device(axes, voltages, filter_taps, delay_plan):
    devices = lax.axis_size(axes[1]) * lax.axis_size(axes[2])
    z = Sizes(voltages, filter_taps, devices, lax.axis_size(axes[2]))
    samples = (
        voltages.astype(jnp.bfloat16)
        .transpose(0, 2, 1, 3)
        .reshape(z.frames_dev, 2 * z.coarse, z.length)
    )
    table = jnp.asarray(dft_columns(z.length, z.chunk, z.flat))
    pieces = z.pieces(0)
    entries = sum(count for _, _, count in pieces)
    plan_rows = -(-2 * len(pieces) // LANES) * LANES
    f32, bf16, i32 = jnp.float32, jnp.bfloat16, jnp.int32
    vmem = pl.BlockSpec(memory_space=pltpu.VMEM)
    return pl.pallas_call(
        functools.partial(kernel, z, axes),
        out_shape=jax.ShapeDtypeStruct((z.block, z.frames), f32),
        in_specs=[vmem, vmem, vmem, pl.BlockSpec(memory_space=pl.ANY)],
        out_specs=vmem,
        scratch_shapes=[
            pltpu.VMEM(table.shape, bf16),
            pltpu.VMEM((z.taps - 1, 2 * z.coarse, z.length), bf16),
            pltpu.VMEM((2 * z.frames_dev * z.coarse, z.length), bf16),
            pltpu.VMEM((z.chunk // LANES, z.frames_dev * z.coarse, LANES), f32),
            pltpu.VMEM((z.channels // z.chunk, 2 * z.frames_dev, z.chunk // 2), bf16),
            pltpu.VMEM((z.devices, 2 * z.frames_dev, z.chunk // 2), bf16),
            pltpu.VMEM((z.frames, z.chunk // z.flat), f32),
            pltpu.VMEM((z.chunk // z.flat, z.frames), f32),
            pltpu.VMEM((z.block // TILE, TILE, z.frames), f32),
            pltpu.VMEM((z.devices, TILE, z.frames), f32),
            pltpu.VMEM((plan_rows, LANES), i32),
            pltpu.VMEM((LANES, plan_rows), i32),
            pltpu.VMEM((entries, TILE, LANES), i32),
            pltpu.VMEM((entries, TILE, LANES), i32),
            pltpu.SemaphoreType.DMA((table.shape[0],)),
            pltpu.SemaphoreType.DMA((2,)),
            pltpu.SemaphoreType.DMA((z.devices,)),
            pltpu.SemaphoreType.DMA((z.devices,)),
            pltpu.SemaphoreType.DMA((z.devices,)),
            pltpu.SemaphoreType.DMA((z.devices,)),
        ],
        compiler_params=pltpu.CompilerParams(
            collective_id=0, has_side_effects=True, vmem_limit_bytes=40 * 2**20
        ),
    )(samples, filter_taps, delay_plan, table)


def solution(mesh):
    axes = ("beam", "freq", "section")
    placed = (P(axes, None, None, None), P(), P())
    return jax.shard_map(
        functools.partial(per_device, axes),
        mesh=mesh,
        in_specs=placed,
        out_specs=P(axes, None),
        check_vma=False,
    )
```

time: 2930 us -> 28.4 us (0.01); the launches traced: 2880 us -> 28.1 us
  local copies, waits for them, and re-layouts: 2790 us -> 4.56 us
  other arithmetic: 42.6 us -> 1.22 us
    gather x5655 -> x0, local copies, waits for them, and re-layouts: 2790 us -> none
where the time goes in v1:
time: 28.4 us; the launch traced here: 28.1 us
  Pallas kernels  22.3 us (79%)
  local copies, waits for them, and re-layouts  4.56 us (16%)
  other arithmetic  1.22 us (4%)
    pallas_call x1, Pallas kernels, per_device(): pl.pallas_call(functools.partial(kernel, z, axes), out_shape=jax.ShapeDty...  22.3 us
    unnamed x7, local copies, waits for them, and re-layouts  4.51 us
    transpose x1, other arithmetic, per_device(): samples = voltages.astype(jnp.bfloat16).transpose(0, 2, 1, 3).reshape(z.f...  1.22 us

profile of v1, /device:TPU:0, one launch (start us, length us, event | category | flops | bytes accessed | tf_op | source)
XLA Modules:
  0.0 28.1 jit_solution(9130408540520592033)
XLA Ops:
  0.0 1.2 %convert_bitcast_fusion = bf16[8,2,8,1024]{3,1,2,0:T(2,128)(2,1)S(1)} fusion(s32[8,8,2,1024]{3,2,1,0:T(2,128)} %param.4), kind=kLoop, calls=%fused_computation.1 | loop fusion | flops 131072 | bytes 786432 | tf_op jit(solution)/shard_map/transpose | solution.py:419
  1.2 0.1 copy.7
  1.3 0.0 copy-start
  1.3 2.2 %copy-done = bf16[4,1024,512]{2,1,0:T(8,128)(2,1)S(1)} copy-done((bf16[4,1024,512]{2,1,0:T(8,128)(2,1)S(1)}, bf16[4,1024,512]{2,1,0:T(8,128)(2,1)}, u32[]{:S(2)}) %copy-start) | copy-done | bytes 4194328
  3.5 0.0 copy-start.1
  3.5 0.9 %copy-done.1 = s32[2,28672]{1,0:T(2,128)S(1)} copy-done((s32[2,28672]{1,0:T(2,128)S(1)}, s32[2,28672]{1,0:T(2,128)}, u32[]{:S(2)}) %copy-start.1) | copy-done | bytes 229400
  4.4 0.0 copy-start.2
  4.4 0.8 %copy-done.2 = f32[8,1024]{1,0:T(8,128)S(1)} copy-done((f32[8,1024]{1,0:T(8,128)S(1)}, f32[8,1024]{1,0:T(8,128)}, u32[]{:S(2)}) %copy-start.2) | copy-done | bytes 32792
  5.2 22.3 %shard_map.46 = f32[128,128]{1,0:T(8,128)S(1)} custom-call(bf16[8,16,1024]{2,1,0:T(8,128)(2,1)S(1)} %bitcast.5, f32[8,1024]{1,0:T(8,128)S(1)} %copy-done.2, s32[2,28672]{1,0:T(2,128)S(1)} %copy-done.1, bf16[4,1024,512]{2,1,0:T(8,128)(2,1)S(1)} %copy-done), custom_call_target="tpu_custom_call" | custom-call | tf_op jit(solution)/shard_map/pallas_call | solution.py:428
  27.5 0.6 %copy.9 = f32[128,128]{1,0:T(8,128)} copy(f32[128,128]{1,0:T(8,128)S(1)} %shard_map.46) | data formatting | bytes 131072
Async XLA Ops:
  1.3 2.2 %copy-start = (bf16[4,1024,512]{2,1,0:T(8,128)(2,1)S(1)}, bf16[4,1024,512]{2,1,0:T(8,128)(2,1)}, u32[]{:S(2)}) copy-start(bf16[4,1024,512]{2,1,0:T(8,128)(2,1)} %constant.2.clone.table_ref) | copy-start | bytes 12582916
  3.5 0.9 %copy-start.1 = (s32[2,28672]{1,0:T(2,128)S(1)}, s32[2,28672]{1,0:T(2,128)}, u32[]{:S(2)}) copy-start(s32[2,28672]{1,0:T(2,128)} %plan_ref.1) | copy-start | bytes 688132
  4.4 0.8 %copy-start.2 = (f32[8,1024]{1,0:T(8,128)S(1)}, f32[8,1024]{1,0:T(8,128)}, u32[]{:S(2)}) copy-start(f32[8,1024]{1,0:T(8,128)} %taps_ref.1) | copy-start | bytes 98308

commit v2 on v1

--- a/solution.py
+++ b/solution.py
@@ -108,11 +108,15 @@
 def kernel(
     z,
     axes,
+    x_hbm,
+    taps_hbm,
+    plan_hbm,
+    table_ref,
+    out_ref,
+    raw,
     x_ref,
     taps_ref,
     plan_ref,
-    table_ref,
-    out_ref,
     table,
     halo,
     lhs,
@@ -127,6 +131,7 @@
     plan_columns,
     upper_plan,
     lower_plan,
+    load_sem,
     table_sem,
     halo_sem,
     send_sem,
@@ -140,6 +145,14 @@
     def at(device):
         return (beam, device // z.sections, lax.rem(device, z.sections))
 
+    voltage_loads = [
+        pltpu.make_async_copy(x_hbm.at[:, :, part], raw.at[part], load_sem.at[part])
+        for part in range(2)
+    ]
+    plan_load = pltpu.make_async_copy(plan_hbm, plan_ref, load_sem.at[2])
+    taps_load = pltpu.make_async_copy(taps_hbm, taps_ref, load_sem.at[3])
+    for load in (*voltage_loads, plan_load, taps_load):
+        load.start()
     loads = []
     for part in range(table_ref.shape[0]):
         loads.append(
@@ -156,6 +169,11 @@
         return carry
 
     lax.fori_loop(1, z.devices, greet, 0)
+    for load in voltage_loads:
+        load.wait()
+    for n in range(z.frames_dev - 1, -1, -1):
+        both = jnp.concatenate([raw[0, n], raw[1, n]], axis=0)
+        x_ref[n] = both.astype(jnp.float32).astype(jnp.bfloat16)
     pl.semaphore_wait(barrier, z.devices - 1)
 
     before = z.taps - 1
@@ -177,6 +195,7 @@
         halo[...] = jnp.zeros_like(halo)
 
     pieces = z.pieces(me)
+    plan_load.wait()
     plan_rows[...] = jnp.zeros_like(plan_rows)
     for piece, (_, start, _) in enumerate(pieces):
         base = pl.multiple_of(start // LANES * LANES, LANES)
@@ -196,6 +215,7 @@
     def _():
         ahead.wait_recv()
 
+    taps_load.wait()
     half = z.coarse
     rows = z.frames_dev * z.coarse
     for lane in range(0, z.length, LANES):
@@ -414,11 +434,6 @@
 def per_device(axes, voltages, filter_taps, delay_plan):
     devices = lax.axis_size(axes[1]) * lax.axis_size(axes[2])
     z = Sizes(voltages, filter_taps, devices, lax.axis_size(axes[2]))
-    samples = (
-        voltages.astype(jnp.bfloat16)
-        .transpose(0, 2, 1, 3)
-        .reshape(z.frames_dev, 2 * z.coarse, z.length)
-    )
     table = jnp.asarray(dft_columns(z.length, z.chunk, z.flat))
     pieces = z.pieces(0)
     entries = sum(count for _, _, count in pieces)
@@ -428,9 +443,13 @@
     return pl.pallas_call(
         functools.partial(kernel, z, axes),
         out_shape=jax.ShapeDtypeStruct((z.block, z.frames), f32),
-        in_specs=[vmem, vmem, vmem, pl.BlockSpec(memory_space=pl.ANY)],
+        in_specs=[pl.BlockSpec(memory_space=pl.ANY)] * 4,
         out_specs=vmem,
         scratch_shapes=[
+            pltpu.VMEM((2, z.frames_dev, z.coarse, z.length), i32),
+            pltpu.VMEM((z.frames_dev, 2 * z.coarse, z.length), bf16),
+            pltpu.VMEM(filter_taps.shape, f32),
+            pltpu.VMEM(delay_plan.shape, i32),
             pltpu.VMEM(table.shape, bf16),
             pltpu.VMEM((z.taps - 1, 2 * z.coarse, z.length), bf16),
             pltpu.VMEM((2 * z.frames_dev * z.coarse, z.length), bf16),
@@ -445,6 +464,7 @@
             pltpu.VMEM((LANES, plan_rows), i32),
             pltpu.VMEM((entries, TILE, LANES), i32),
             pltpu.VMEM((entries, TILE, LANES), i32),
+            pltpu.SemaphoreType.DMA((4,)),
             pltpu.SemaphoreType.DMA((table.shape[0],)),
             pltpu.SemaphoreType.DMA((2,)),
             pltpu.SemaphoreType.DMA((z.devices,)),
@@ -453,9 +473,9 @@
             pltpu.SemaphoreType.DMA((z.devices,)),
         ],
         compiler_params=pltpu.CompilerParams(
-            collective_id=0, has_side_effects=True, vmem_limit_bytes=40 * 2**20
+            collective_id=0, has_side_effects=True, vmem_limit_bytes=63 * 2**20
         ),
-    )(samples, filter_taps, delay_plan, table)
+    )(voltages, filter_taps, delay_plan, table)
 
 
 def solution(mesh):

time: 28.4 us -> 24.3 us (0.86)
  local copies, waits for them, and re-layouts: 4.56 us -> 1.47 us
  other arithmetic: 1.22 us -> 0 us
  Pallas kernels: 22.3 us -> 22.6 us
    unnamed x7 -> x1, local copies, waits for them, and re-layouts: 4.51 us -> 1.47 us
    transpose x1 -> x0, other arithmetic: 1.22 us -> none  [per_device(): samples = voltages.astype(jnp.bfloat16).transpose(0, 2, 1, 3).reshape(z.f...]
    pallas_call x1, Pallas kernels: 22.3 us -> 22.6 us  [per_device(): pl.pallas_call(functools.partial(kernel, z, axes), out_shape=jax.ShapeDty...]
where the time goes in v2:
time: 24.3 us; the launch traced here: 24.1 us
  Pallas kernels  22.6 us (93%)
  local copies, waits for them, and re-layouts  1.47 us (6%)
    pallas_call x1, Pallas kernels, per_device(): pl.pallas_call(functools.partial(kernel, z, axes), out_shape=jax.ShapeDty...  22.6 us
    unnamed x1, local copies, waits for them, and re-layouts  1.47 us

profile of v2, /device:TPU:0, one launch (start us, length us, event | category | flops | bytes accessed | tf_op | source)
XLA Modules:
  0.0 24.1 jit_solution(8566917294905741126)
XLA Ops:
  0.0 22.6 %shard_map.46 = f32[128,128]{1,0:T(8,128)} custom-call(s32[8,8,2,1024]{3,2,1,0:T(2,128)} %x_hbm.1, f32[8,1024]{1,0:T(8,128)} %taps_hbm.1, s32[2,28672]{1,0:T(2,128)} %plan_hbm.1, bf16[4,1024,512]{2,1,0:T(8,128)(2,1)} %constant.2.clone.table_ref), custom_call_target="tpu_custom_call" | custom-call | tf_op jit(solution)/shard_map/pallas_call | solution.py:443
  22.7 1.5 %copy.6 = f32[128,128]{1,0:T(8,128)} copy(f32[128,128]{1,0:T(8,128)} %shard_map.46) | data formatting | bytes 131072

commit v3 on v2

--- a/solution.py
+++ b/solution.py
@@ -171,24 +171,32 @@
     lax.fori_loop(1, z.devices, greet, 0)
     for load in voltage_loads:
         load.wait()
-    for n in range(z.frames_dev - 1, -1, -1):
-        both = jnp.concatenate([raw[0, n], raw[1, n]], axis=0)
-        x_ref[n] = both.astype(jnp.float32).astype(jnp.bfloat16)
-    pl.semaphore_wait(barrier, z.devices - 1)
 
     before = z.taps - 1
-    ahead = pltpu.make_async_remote_copy(
-        src_ref=x_ref.at[pl.ds(z.frames_dev - before, before)],
-        dst_ref=halo,
-        send_sem=halo_sem.at[0],
-        recv_sem=halo_sem.at[1],
-        device_id=at(lax.rem(me + 1, z.devices)),
-        device_id_type=MESH,
-    )
-
-    @pl.when(me < z.devices - 1)
-    def _():
-        ahead.start()
+    ahead = []
+    for piece in range(z.length // COLUMNS):
+        lanes = pl.ds(piece * COLUMNS, COLUMNS)
+        ahead.append(
+            pltpu.make_async_remote_copy(
+                src_ref=x_ref.at[pl.ds(z.frames_dev - before, before), :, lanes],
+                dst_ref=halo.at[:, :, lanes],
+                send_sem=halo_sem.at[0, piece],
+                recv_sem=halo_sem.at[1, piece],
+                device_id=at(lax.rem(me + 1, z.devices)),
+                device_id_type=MESH,
+            )
+        )
+    for piece, copy in enumerate(ahead):
+        lanes = slice(piece * COLUMNS, (piece + 1) * COLUMNS)
+        for n in range(z.frames_dev):
+            both = jnp.concatenate([raw[0, n, :, lanes], raw[1, n, :, lanes]], axis=0)
+            x_ref[n, :, lanes] = both.astype(jnp.float32).astype(jnp.bfloat16)
+        if piece == 0:
+            pl.semaphore_wait(barrier, z.devices - 1)
+
+        @pl.when(me < z.devices - 1)
+        def _():
+            copy.start()
 
     @pl.when(me == 0)
     def _():
@@ -211,15 +219,17 @@
             lower_plan[entry] = jnp.broadcast_to(both[:, 1:2], (TILE, LANES))
             entry += 1
 
-    @pl.when(me > 0)
-    def _():
-        ahead.wait_recv()
-
     taps_load.wait()
     half = z.coarse
     rows = z.frames_dev * z.coarse
     for lane in range(0, z.length, LANES):
         lanes = slice(lane, lane + LANES)
+        if lane % COLUMNS == 0:
+
+            @pl.when(me > 0)
+            def _():
+                ahead[lane // COLUMNS].wait_recv()
+
         window = [halo[n, :, lanes].astype(jnp.float32) for n in range(before)]
         window += [x_ref[n, :, lanes].astype(jnp.float32) for n in range(z.frames_dev)]
         taps = [taps_ref[j : j + 1, lanes] for j in range(z.taps)]
@@ -406,7 +416,8 @@
 
     @pl.when(me < z.devices - 1)
     def _():
-        ahead.wait_send()
+        for copy in ahead:
+            copy.wait_send()
 
     def finish(step, carry):
         device = lax.rem(me + step, z.devices)
@@ -466,7 +477,7 @@
             pltpu.VMEM((entries, TILE, LANES), i32),
             pltpu.SemaphoreType.DMA((4,)),
             pltpu.SemaphoreType.DMA((table.shape[0],)),
-            pltpu.SemaphoreType.DMA((2,)),
+            pltpu.SemaphoreType.DMA((2, z.length // COLUMNS)),
             pltpu.SemaphoreType.DMA((z.devices,)),
             pltpu.SemaphoreType.DMA((z.devices,)),
             pltpu.SemaphoreType.DMA((z.devices,)),

time: 24.3 us -> 24.1 us (level)
  no operation moved by 1% of the time
where the time goes in v3:
time: 24.1 us; the launch traced here: 24 us
  Pallas kernels  22.5 us (93%)
  local copies, waits for them, and re-layouts  1.47 us (6%)
    pallas_call x1, Pallas kernels, per_device(): pl.pallas_call(functools.partial(kernel, z, axes), out_shape=jax.ShapeDty...  22.5 us
    unnamed x1, local copies, waits for them, and re-layouts  1.47 us

profile of v3, /device:TPU:0, one launch (start us, length us, event | category | flops | bytes accessed | tf_op | source)
XLA Modules:
  0.0 24.0 jit_solution(7877039984986937008)
XLA Ops:
  0.0 22.5 %shard_map.46 = f32[128,128]{1,0:T(8,128)} custom-call(s32[8,8,2,1024]{3,2,1,0:T(2,128)} %x_hbm.1, f32[8,1024]{1,0:T(8,128)} %taps_hbm.1, s32[2,28672]{1,0:T(2,128)} %plan_hbm.1, bf16[4,1024,512]{2,1,0:T(8,128)(2,1)} %constant.2.clone.table_ref), custom_call_target="tpu_custom_call" | custom-call | tf_op jit(solution)/shard_map/pallas_call | solution.py:454
  22.5 1.5 %copy.6 = f32[128,128]{1,0:T(8,128)} copy(f32[128,128]{1,0:T(8,128)} %shard_map.46) | data formatting | bytes 131072

commit v4 on v3

--- a/solution.py
+++ b/solution.py
@@ -282,7 +282,7 @@
                 )
 
         def send(step, carry):
-            c = lax.rem(step + me // (z.share * per_coarse), z.coarse)
+            c = lax.rem(step + z.coarse // 2 + me // (z.share * per_coarse), z.coarse)
             chunk = c * per_coarse + position
             for twin in range(z.share):
                 device = chunk * z.share + twin
@@ -370,7 +370,8 @@
         state[k] = tile
 
     def deliver(step, carry):
-        device = lax.rem(me + step, z.devices)
+        far = (step + 1) // 2 * (1 - 2 * lax.rem(step, 2))
+        device = lax.rem(me + z.devices // 2 + far + z.devices, z.devices)
         pltpu.make_async_remote_copy(
             src_ref=state.at[z.first_tile(device, z.local_levels)],
             dst_ref=tiles_in.at[me],
@@ -381,7 +382,7 @@
         ).start()
         return carry
 
-    lax.fori_loop(1, z.devices, deliver, 0)
+    lax.fori_loop(0, z.devices - 1, deliver, 0)
     tiles_in[me] = state[z.first_tile(me, z.local_levels)]
 
     def accept(step, carry):

time: 24.1 us -> 24.6 us (1.021)
  Pallas kernels: 22.5 us -> 23 us
    pallas_call x1, Pallas kernels: 22.5 us -> 23 us  [per_device(): pl.pallas_call(functools.partial(kernel, z, axes), out_shape=jax.ShapeDty...]
where the time goes in v4:
time: 24.6 us; the launch traced here: 24.5 us
  Pallas kernels  23 us (93%)
  local copies, waits for them, and re-layouts  1.47 us (6%)
    pallas_call x1, Pallas kernels, per_device(): pl.pallas_call(functools.partial(kernel, z, axes), out_shape=jax.ShapeDty...  23 us
    unnamed x1, local copies, waits for them, and re-layouts  1.47 us

profile of v4, /device:TPU:0, one launch (start us, length us, event | category | flops | bytes accessed | tf_op | source)
XLA Modules:
  0.0 24.5 jit_solution(18345045356448301476)
XLA Ops:
  0.0 23.0 %shard_map.46 = f32[128,128]{1,0:T(8,128)} custom-call(s32[8,8,2,1024]{3,2,1,0:T(2,128)} %x_hbm.1, f32[8,1024]{1,0:T(8,128)} %taps_hbm.1, s32[2,28672]{1,0:T(2,128)} %plan_hbm.1, bf16[4,1024,512]{2,1,0:T(8,128)(2,1)} %constant.2.clone.table_ref), custom_call_target="tpu_custom_call" | custom-call | tf_op jit(solution)/shard_map/pallas_call | solution.py:455
  23.0 1.5 %copy.6 = f32[128,128]{1,0:T(8,128)} copy(f32[128,128]{1,0:T(8,128)} %shard_map.46) | data formatting | bytes 131072
